TPU v7x, 32 devices: a whole 2x2x4 slice. The times are simulated.
32 devices in a mesh: phase: 4 (over y, x), tile: 4 (over z), dp: 2 (over core).
Axes of the slice: x: 2, y: 2, z: 4, core: 2. Of those that a mesh axis runs over, the one named last changes fastest.
Arguments:
- camera_feats: bfloat16 [4, 2, 3, 4, 176, 128], P(None, 'dp', None, 'tile'), may hold values from -6 to 6
- backbone_w: bfloat16 [4, 1152, 128], P('phase'), may hold values from -0.1875 to 0.1875
- depth_w: bfloat16 [128, 118], replicated, may hold values from -1 to 1
- block_tile: int32 [4, 2, 1056, 1], P('phase', 'dp', 'tile'), may hold values from 0 to 3; in each aligned block of 264 rows (0 to 263, 264 to 527, ..., all dimensions but the last counted through in order) at most 264 rows name the same one
- point_slot: int32 [4, 2, 1056, 236], P('phase', 'dp', 'tile'), may hold values from 0 to 15
- block_cells: int32 [4, 2, 1056, 16], P('phase', 'dp', 'tile'), may hold values from 0 to 1024, as said below
- bev_w: bfloat16 [1152, 128], replicated, may hold values from -0.1875 to 0.1875
- cotangent: bfloat16 [4, 2, 16, 256, 128], P('phase', 'dp', 'tile'), may hold values from -6 to 6
Outputs:
- encoded: bfloat16 [4, 2, 16, 256, 128], P('phase', 'dp', 'tile')
- conv_grad: float32 [128, 1152], P('tile')
Inputs may be any that keep to these rules, and one draw needn't show every extreme that they name: `block_tile`: among the 264 blocks of one sample on one index of tile (an aligned run of rows), at most 264 name the same tile. `block_cells`: 1024 marks a slot whose cell lies outside the grid.
All inputs are finite; a program needn't handle non-finite values.
Results may differ from a plain program's by a relative error of at most 0.0085.
Values may be sent and summed in bfloat16 or wider, within the bound.
A program may use at most 64 MiB of HBM per device.

v0:
```python
import jax
import jax.numpy as jnp
from jax import lax
from jax.sharding import PartitionSpec as P

NSEG = 2
BLK = 4
BOUND = 8.0


def extended(cells, sides, width):
    for axis, dim in sides:
        count = lax.axis_size(axis)
        ends = count - 1
        head = lax.slice_in_dim(cells, 0, width, axis=dim)
        tail = lax.slice_in_dim(cells, cells.shape[dim] - width, cells.shape[dim], axis=dim)
        cells = jnp.concatenate(
            [
                lax.ppermute(tail, axis, [(i, (i + 1) % count) for i in range(ends)]),
                cells,
                lax.ppermute(head, axis, [((i + 1) % count, i) for i in range(ends)]),
            ],
            axis=dim,
        )
    return cells


def passed_along(block, axis, distance):
    devices = range(lax.axis_size(axis))
    route = [(i - distance, i) for i in devices if i - distance in devices]
    return lax.ppermute(block, axis, route)


def from_root(block, axis, source):
    block = jnp.where(lax.axis_index(axis) == source, block, jnp.zeros_like(block))
    return lax.psum(block, axis)


def patches_from(padded, row_count, col_count):
    widened = jnp.pad(padded, [(0, 0)] * (padded.ndim - 2) + [(1, 1), (0, 0)])
    shifted = [
        widened[..., row_off : row_off + row_count, col_off : col_off + col_count, :]
        for row_off in range(3)
        for col_off in range(3)
    ]
    stacked = jnp.concatenate(shifted, axis=-1)
    return stacked.reshape(-1, stacked.shape[-1])


def section(images, weight):
    padded = extended(images, (("tile", 2),), 1)
    hidden = jnp.dot(
        patches_from(padded, images.shape[2], images.shape[3]),
        weight,
        preferred_element_type=jnp.float32,
    ).reshape(images.shape)
    return (images.astype(jnp.float32) + jax.nn.silu(hidden)).astype(jnp.bfloat16)


def body(camera_feats, backbone_w, depth_w, block_tile, point_slot, block_cells, bev_w, cotangent):
    phases = lax.axis_size("phase")
    phase_idx = lax.axis_index("phase")
    tile_count = lax.axis_size("tile")
    micro_all = camera_feats.shape[0]
    per_phase = micro_all // phases
    own_weight = backbone_w[0]
    carried = jnp.zeros_like(camera_feats[0])
    collected = jnp.zeros_like(camera_feats)
    steps_total = micro_all + phases - 1
    for step_idx in range(steps_total):
        if step_idx < micro_all:
            entering = jnp.where(phase_idx == 0, camera_feats[step_idx], carried)
        else:
            entering = carried
        leaving = section(entering, own_weight)
        finished = step_idx - (phases - 1)
        if finished >= 0:
            collected = collected.at[finished].set(
                jnp.where(phase_idx == phases - 1, leaving, collected[finished])
            )
        if step_idx + 1 < steps_total:
            carried = passed_along(leaving, "phase", 1)
    everything = from_root(collected, "phase", phases - 1)
    own_feats = lax.dynamic_slice_in_dim(everything, phase_idx * per_phase, per_phase, 0)
    samples_dev = own_feats.shape[0] * own_feats.shape[1]
    channels = own_feats.shape[-1]
    context = own_feats.reshape(samples_dev, -1, channels)
    positions = context.shape[1]
    seg_len = depth_w.shape[1] // NSEG
    slot_total = block_cells.shape[-1]
    pos_groups = positions // BLK
    block_count = pos_groups * NSEG
    logits = jnp.dot(context.reshape(-1, channels), depth_w, preferred_element_type=jnp.float32)
    depth_prob = jax.nn.softmax(BOUND * jnp.tanh(logits / BOUND), axis=-1)
    depth_blocks = (
        depth_prob.reshape(samples_dev, pos_groups, BLK, NSEG, seg_len)
        .transpose(0, 1, 3, 2, 4)
        .reshape(samples_dev, block_count, BLK, seg_len)
    )
    slot_blocks = point_slot.reshape(samples_dev, block_count, BLK, seg_len)
    splat_w = jnp.stack(
        [
            jnp.sum(
                jnp.where(slot_blocks == target, depth_blocks, jnp.zeros_like(depth_blocks)),
                axis=-1,
            )
            for target in range(slot_total)
        ],
        axis=2,
    ).astype(jnp.bfloat16)
    block_ctx = jnp.repeat(context.reshape(samples_dev, pos_groups, BLK, channels), NSEG, axis=1)
    row_count = cotangent.shape[2]
    col_count = cotangent.shape[3]
    cells_tile = row_count * col_count
    capacity = max(2, 4 * block_count // tile_count)
    targets = block_tile.reshape(samples_dev, block_count)
    member = (targets[..., None] == jnp.arange(tile_count, dtype=jnp.int32)).astype(jnp.int32)
    slot_rank = jnp.sum((jnp.cumsum(member, axis=1) - 1) * member, axis=-1)
    slot_flat = targets * capacity + slot_rank
    sample_rows = jnp.broadcast_to(
        jnp.arange(samples_dev, dtype=jnp.int32)[:, None], slot_flat.shape
    )
    send_ctx = (
        jnp.zeros((samples_dev, tile_count * capacity, BLK, channels), jnp.bfloat16)
        .at[sample_rows, slot_flat]
        .set(block_ctx)
    )
    send_weights = (
        jnp.zeros((samples_dev, tile_count * capacity, slot_total, BLK), jnp.bfloat16)
        .at[sample_rows, slot_flat]
        .set(splat_w)
    )
    send_cells = (
        jnp.full((samples_dev, tile_count * capacity, slot_total), cells_tile, jnp.int32)
        .at[sample_rows, slot_flat]
        .set(block_cells.reshape(samples_dev, block_count, slot_total))
    )
    send_ctx = send_ctx.reshape(samples_dev, tile_count, capacity, BLK, channels)
    send_weights = send_weights.reshape(samples_dev, tile_count, capacity, slot_total, BLK)
    send_cells = send_cells.reshape(samples_dev, tile_count, capacity, slot_total)
    got_ctx, got_weights, got_cells = (
        lax.all_to_all(send_ctx, "tile", split_axis=1, concat_axis=1, tiled=True),
        lax.all_to_all(send_weights, "tile", split_axis=1, concat_axis=1, tiled=True),
        lax.all_to_all(send_cells, "tile", split_axis=1, concat_axis=1, tiled=True),
    )
    pooled = jnp.einsum(
        "ankti,ankic->anktc", got_weights, got_ctx, preferred_element_type=jnp.float32
    ).astype(jnp.bfloat16)
    group_size = min(8, tile_count)
    group_count = tile_count // group_size
    group_rows = group_size * capacity * slot_total
    pooled_groups = jnp.moveaxis(
        pooled.reshape(samples_dev, group_count, group_rows, channels), 1, 0
    )
    cell_groups = jnp.moveaxis(got_cells.reshape(samples_dev, group_count, group_rows), 1, 0)
    cell_range = jnp.arange(cells_tile, dtype=jnp.int32).reshape(1, cells_tile, 1)

    def splat_group(grid_sum, pieces):
        part_pooled, part_cells = pieces
        one_hot = (part_cells[:, None, :] == cell_range).astype(jnp.bfloat16)
        grid_sum = grid_sum + jnp.einsum(
            "sxr,src->sxc", one_hot, part_pooled, preferred_element_type=jnp.float32
        )
        return (grid_sum, None)

    totals, _ = lax.scan(
        splat_group,
        jnp.zeros((samples_dev, cells_tile, channels), jnp.float32),
        (pooled_groups, cell_groups),
    )
    bev_grid = totals.astype(jnp.bfloat16).reshape(samples_dev, row_count, col_count, channels)
    padded_grid = extended(bev_grid, (("tile", 1),), 1)
    bev_patches = patches_from(padded_grid, row_count, col_count)
    mixed = jnp.dot(bev_patches, bev_w, preferred_element_type=jnp.float32)
    encoded = (
        (bev_grid.astype(jnp.float32).reshape(-1, channels) + mixed)
        .astype(jnp.bfloat16)
        .reshape(cotangent.shape)
    )
    upstream = cotangent.reshape(-1, channels)
    total_cells = (
        micro_all * cotangent.shape[1] * lax.axis_size("dp") * row_count * tile_count * col_count
    )
    grad_scale = float(total_cells) ** (-0.5)
    grad_share = lax.psum_scatter(
        grad_scale
        * lax.dot_general(
            upstream, bev_patches, (((0,), (0,)), ((), ())), preferred_element_type=jnp.float32
        ),
        "tile",
        scatter_dimension=0,
        tiled=True,
    )
    conv_grad = lax.psum(grad_share, ("phase", "dp"))
    return (encoded, conv_grad)


def solution(mesh):
    return jax.shard_map(
        body,
        mesh=mesh,
        in_specs=(
            P(None, "dp", None, "tile", None, None),
            P("phase", None, None),
            P(),
            P("phase", "dp", "tile", None),
            P("phase", "dp", "tile", None),
            P("phase", "dp", "tile", None),
            P(),
            P("phase", "dp", "tile", None, None),
        ),
        out_specs=(P("phase", "dp", "tile", None, None), P("tile", None)),
        check_vma=False,
    )
```

profile of v0, /device:TPU:0, one launch (start us, length us, event | category | flops | bytes accessed | tf_op | source)
XLA Modules:
  0.0 385.2 jit_solution(11881665665288128379)
XLA Ops:
  8.2 4.9 %collective-permute-start = (bf16[1,3,1,176,128]{4,3,1,2,0:T(8,128)(2,1)S(1)}, bf16[1,3,1,176,128]{4,3,1,2,0:T(8,128)(2,1)S(1)}, u32[]{:S(2)}, u32[]{:S(2)}) collective-permute-start(bf16[1,3,1,176,128]{4,3,1,2,0:T(8,128)(2,1)S(1)} %fusion.83), channel_id=1, source_target_pairs={{0,2},{2,4},{4,6},{1,3},{3,5},{5,7},{8,10},{10,12},{12,14},{9,11},... | collective-permute-start | bytes 405512 | tf_op jit(solution)/shard_map/ppermute | solution.py:19
  33.8 4.4 %collective-permute-done.4 = bf16[1,3,1,176,128]{4,3,1,2,0:T(8,128)(2,1)S(1)} collective-permute-done((bf16[1,3,1,176,128]{4,3,1,2,0:T(8,128)(2,1)S(1)}, bf16[1,3,1,176,128]{4,3,1,2,0:T(8,128)(2,1)S(1)}, u32[]{:S(2)}, u32[]{:S(2)}) %collective-permute-start.4) | collective-permute-done | bytes 135200 | tf_op jit(solution)/shard_map/ppermute | solution.py:21
  39.3 4.4 %collective-permute-start.5 = (bf16[1,3,1,176,128]{4,3,1,2,0:T(8,128)(2,1)S(1)}, bf16[1,3,1,176,128]{4,3,1,2,0:T(8,128)(2,1)S(1)}, u32[]{:S(2)}, u32[]{:S(2)}) collective-permute-start(bf16[1,3,1,176,128]{4,3,1,2,0:T(8,128)(2,1)S(1)} %add_convert_fusion.5), channel_id=1, source_target_pairs={{0,8},{8,16},{16,24},{1,9},{9,17},{17,25},{2,10},{10,18},{18,26},{... | collective-permute-start | bytes 405512 | tf_op jit(solution)/shard_map/ppermute | solution.py:31
  52.3 4.4 %collective-permute-done.7 = bf16[1,3,1,176,128]{4,3,1,2,0:T(8,128)(2,1)S(1)} collective-permute-done((bf16[1,3,1,176,128]{4,3,1,2,0:T(8,128)(2,1)S(1)}, bf16[1,3,1,176,128]{4,3,1,2,0:T(8,128)(2,1)S(1)}, u32[]{:S(2)}, u32[]{:S(2)}) %collective-permute-start.7) | collective-permute-done | bytes 135200 | tf_op jit(solution)/shard_map/ppermute | solution.py:21
  57.8 4.4 %collective-permute-start.8 = (bf16[1,3,1,176,128]{4,3,1,2,0:T(8,128)(2,1)S(1)}, bf16[1,3,1,176,128]{4,3,1,2,0:T(8,128)(2,1)S(1)}, u32[]{:S(2)}, u32[]{:S(2)}) collective-permute-start(bf16[1,3,1,176,128]{4,3,1,2,0:T(8,128)(2,1)S(1)} %add_convert_fusion.4), channel_id=1, source_target_pairs={{0,8},{8,16},{16,24},{1,9},{9,17},{17,25},{2,10},{10,18},{18,26},{... | collective-permute-start | bytes 405512 | tf_op jit(solution)/shard_map/ppermute | solution.py:31
  66.1 4.6 %collective-permute-start.9 = (bf16[1,3,1,176,128]{4,3,1,2,0:T(8,128)(2,1)S(1)}, bf16[1,3,1,176,128]{4,3,1,2,0:T(8,128)(2,1)S(1)}, u32[]{:S(2)}, u32[]{:S(2)}) collective-permute-start(bf16[1,3,1,176,128]{4,3,1,2,0:T(8,128)(2,1)S(1)} %fusion.57), channel_id=1, source_target_pairs={{0,2},{2,4},{4,6},{1,3},{3,5},{5,7},{8,10},{10,12},{12,14},{9,11},... | collective-permute-start | bytes 405512 | tf_op jit(solution)/shard_map/ppermute | solution.py:19
  74.4 5.2 %collective-permute-start.11 = (bf16[1,3,1,176,128]{4,3,1,2,0:T(8,128)(2,1)S(1)}, bf16[1,3,1,176,128]{4,3,1,2,0:T(8,128)(2,1)S(1)}, u32[]{:S(2)}, u32[]{:S(2)}) collective-permute-start(bf16[1,3,1,176,128]{4,3,1,2,0:T(8,128)(2,1)S(1)} %get-tuple-element.92), channel_id=1, source_target_pairs={{0,8},{8,16},{16,24},{1,9},{9,17},{17,25},{2,10},{10,18},{18,26},{... | collective-permute-start | bytes 405512 | tf_op jit(solution)/shard_map/ppermute | solution.py:31
  82.1 4.4 %collective-permute-start.12 = (bf16[1,3,1,176,128]{4,3,1,2,0:T(8,128)(2,1)S(1)}, bf16[1,3,1,176,128]{4,3,1,2,0:T(8,128)(2,1)S(1)}, u32[]{:S(2)}, u32[]{:S(2)}) collective-permute-start(bf16[1,3,1,176,128]{4,3,1,2,0:T(8,128)(2,1)S(1)} %collective-permute-done.11), channel_id=1, source_target_pairs={{0,2},{2,4},{4,6},{1,3},{3,5},{5,7},{8,10},{10,12},{12,14},{9,11},... | collective-permute-start | bytes 405512 | tf_op jit(solution)/shard_map/ppermute | solution.py:19
  89.0 4.4 %collective-permute-done.13 = bf16[1,3,1,176,128]{4,3,1,2,0:T(8,128)(2,1)S(1)} collective-permute-done((bf16[1,3,1,176,128]{4,3,1,2,0:T(8,128)(2,1)S(1)}, bf16[1,3,1,176,128]{4,3,1,2,0:T(8,128)(2,1)S(1)}, u32[]{:S(2)}, u32[]{:S(2)}) %collective-permute-start.13) | collective-permute-done | bytes 135200 | tf_op jit(solution)/shard_map/ppermute | solution.py:21
  94.6 5.3 %collective-permute-start.14 = (bf16[1,3,1,176,128]{4,3,1,2,0:T(8,128)(2,1)S(1)}, bf16[1,3,1,176,128]{4,3,1,2,0:T(8,128)(2,1)S(1)}, u32[]{:S(2)}, u32[]{:S(2)}) collective-permute-start(bf16[1,3,1,176,128]{4,3,1,2,0:T(8,128)(2,1)S(1)} %get-tuple-element.90), channel_id=1, source_target_pairs={{0,8},{8,16},{16,24},{1,9},{9,17},{17,25},{2,10},{10,18},{18,26},{... | collective-permute-start | bytes 405512 | tf_op jit(solution)/shard_map/ppermute | solution.py:31
  107.1 4.1 %collective-permute-done.16 = bf16[1,3,1,176,128]{4,3,1,2,0:T(8,128)(2,1)S(1)} collective-permute-done((bf16[1,3,1,176,128]{4,3,1,2,0:T(8,128)(2,1)S(1)}, bf16[1,3,1,176,128]{4,3,1,2,0:T(8,128)(2,1)S(1)}, u32[]{:S(2)}, u32[]{:S(2)}) %collective-permute-start.16) | collective-permute-done | bytes 135200 | tf_op jit(solution)/shard_map/ppermute | solution.py:21
  112.4 5.3 %collective-permute-start.17 = (bf16[1,3,1,176,128]{4,3,1,2,0:T(8,128)(2,1)S(1)}, bf16[1,3,1,176,128]{4,3,1,2,0:T(8,128)(2,1)S(1)}, u32[]{:S(2)}, u32[]{:S(2)}) collective-permute-start(bf16[1,3,1,176,128]{4,3,1,2,0:T(8,128)(2,1)S(1)} %get-tuple-element.88), channel_id=1, source_target_pairs={{0,8},{8,16},{16,24},{1,9},{9,17},{17,25},{2,10},{10,18},{18,26},{... | collective-permute-start | bytes 405512 | tf_op jit(solution)/shard_map/ppermute | solution.py:31
  124.7 4.4 %collective-permute-done.19 = bf16[1,3,1,176,128]{4,3,1,2,0:T(8,128)(2,1)S(1)} collective-permute-done((bf16[1,3,1,176,128]{4,3,1,2,0:T(8,128)(2,1)S(1)}, bf16[1,3,1,176,128]{4,3,1,2,0:T(8,128)(2,1)S(1)}, u32[]{:S(2)}, u32[]{:S(2)}) %collective-permute-start.19) | collective-permute-done | bytes 135200 | tf_op jit(solution)/shard_map/ppermute | solution.py:21
  141.2 36.8 %all-reduce.14.cloned.1.call-done = bf16[4,1,3,1,176,128]{5,4,2,3,1,0:T(8,128)(2,1)} async-done(((bf16[4,1,3,1,176,128]{5,4,2,3,1,0:T(8,128)(2,1)}), bf16[4,1,3,1,176,128]{5,4,2,3,1,0:T(8,128)(2,1)}) %all-reduce.14.cloned.1.call-update) | async-done | bytes 540688 | tf_op jit(solution)/shard_map/psum | solution.py:36
  180.1 7.7 %fusion.26 = (bf16[132,2,4]{2,1,0:T(2,128)(2,1)S(1)}, bf16[132,2,4]{2,1,0:T(2,128)(2,1)S(1)}, bf16[132,2,4]{2,1,0:T(2,128)(2,1)S(1)}, bf16[132,2,4]{2,1,0:T(2,12...) fusion(pred[1,132,2,4,59]{4,3,2,1,0:T(4,128)(4,1)S(1)} %eq.411,, ...), kind=kLoop, calls=%fused_computation.54 | loop fusion | flops 1976832 | bytes 1279872 | tf_op jit(solution)/shard_map/reduce_sum | solution.py:103
  202.1 8.6 %scatter_fusion = bf16[1056,16,4]{1,2,0:T(4,128)(2,1)S(1)} fusion(bf16[1056,16,4]{1,2,0:T(4,128)(2,1)S(1)} %broadcast.618, s32[264]{0:T(512)S(1)} %fusion.62, bf16[264,16,4]{1,2,0:T(4,128)(2,1)S(1)} %copy.70), kind=kCustom, calls=%fused_computation.1 | custom fusion | bytes 102432 | tf_op jit(solution)/shard_map/scatter | solution.py:131
  212.0 4.6 %all-to-all-start.1 = ((bf16[1,4,264,16,4]{2,3,4,0,1:T(8,128)(2,1)}), bf16[1,4,264,16,4]{2,3,4,0,1:T(8,128)(2,1)S(1)}, u32[]{:S(2)}, u32[]{:S(2)}) async-start(bf16[1,4,264,16,4]{2,3,4,0,1:T(8,128)(2,1)} %copy.71), calls=%async_computation.1 | async-start | bytes 393216 | tf_op jit(solution)/shard_map/all_to_all | solution.py:143
  217.8 26.7 %scatter_fusion.1 = bf16[1056,4,128]{2,1,0:T(4,128)(2,1)} fusion(bf16[1056,4,128]{2,1,0:T(4,128)(2,1)} %broadcast.620, s32[264]{0:T(512)S(1)} %fusion.62, bf16[264,4,128]{2,1,0:T(4,128)(2,1)S(1)} %bitcast.272), kind=kCustom, calls=%fused_computation.2 | custom fusion | bytes 812064 | tf_op jit(solution)/shard_map/scatter | solution.py:126
  244.6 5.1 %all-to-all-start.2 = ((bf16[1,4,264,4,128]{4,3,2,0,1:T(4,128)(2,1)}), bf16[1,4,264,4,128]{4,3,2,0,1:T(4,128)(2,1)S(1)}, u32[]{:S(2)}, u32[]{:S(2)}) async-start(bf16[1,4,264,4,128]{4,3,2,0,1:T(4,128)(2,1)} %bitcast.70), calls=%async_computation.2 | async-start | bytes 2162688 | tf_op jit(solution)/shard_map/all_to_all | solution.py:142
  250.8 24.5 %all-to-all-done.2 = bf16[1,4,264,4,128]{4,3,2,0,1:T(4,128)(2,1)S(1)} async-done(((bf16[1,4,264,4,128]{4,3,2,0,1:T(4,128)(2,1)}), bf16[1,4,264,4,128]{4,3,2,0,1:T(4,128)(2,1)S(1)}, u32[]{:S(2)}, u32[]{:S(2)}) %all-to-all-start.2) | async-done | bytes 1081376 | tf_op jit(solution)/shard_map/all_to_all | solution.py:142
  277.0 10.5 %fusion.4 = bf16[1024,128]{1,0:T(8,128)(2,1)S(1)} fusion(bf16[16896,128]{1,0:T(8,128)(2,1)S(1)} %bitcast.247, s32[16896]{0:T(1024)S(1)} %eq.358), kind=kOutput, calls=%fused_computation.15 | convolution fusion | flops 4446617600 | bytes 4655104 | tf_op jit(solution)/shard_map/while/body/eval_jaxpr/sxr,src->sxc/dot_general | solution.py:161
  290.8 4.3 %collective-permute-done.21 = bf16[1,1,256,128]{3,2,1,0:T(8,128)(2,1)S(1)} collective-permute-done((bf16[1,1,256,128]{3,2,1,0:T(8,128)(2,1)S(1)}, bf16[1,1,256,128]{3,2,1,0:T(8,128)(2,1)S(1)}, u32[]{:S(2)}, u32[]{:S(2)}) %collective-permute-start.21) | collective-permute-done | bytes 65568 | tf_op jit(solution)/shard_map/ppermute | solution.py:21
  298.7 21.6 %reduce-scatter.4.cloned.1.call-done = f32[32,1152]{1,0:T(8,128)} async-done(((f32[128,1152]{1,0:T(8,128)}), f32[32,1152]{1,0:T(8,128)}) %reduce-scatter.4.cloned.1.call-update) | async-done | bytes 147472
  323.7 53.0 %all-reduce.16.cloned.1.call-done = f32[32,1152]{0,1:T(8,128)} async-done(((f32[32,1152]{0,1:T(8,128)}), f32[32,1152]{0,1:T(8,128)}) %all-reduce.16.cloned.1.call-update) | async-done | bytes 147472 | tf_op jit(solution)/shard_map/psum | solution.py:194
  (232 shorter events, 106.9 us)
Async XLA Ops:
  7.2 170.8 %all-reduce.14.cloned.1.call-start = ((), (), s32[]{:S(2)}) async-start(), calls=%async_computation.4 | async-start | bytes 1081344 | tf_op jit(solution)/shard_map/psum | solution.py:36
  8.2 7.8 %collective-permute-start = (bf16[1,3,1,176,128]{4,3,1,2,0:T(8,128)(2,1)S(1)}, bf16[1,3,1,176,128]{4,3,1,2,0:T(8,128)(2,1)S(1)}, u32[]{:S(2)}, u32[]{:S(2)}) collective-permute-start(bf16[1,3,1,176,128]{4,3,1,2,0:T(8,128)(2,1)S(1)} %fusion.83), channel_id=1, source_target_pairs={{0,2},{2,4},{4,6},{1,3},{3,5},{5,7},{8,10},{10,12},{12,14},{9,11},... | collective-permute-start | bytes 405512 | tf_op jit(solution)/shard_map/ppermute | solution.py:19
  13.1 6.9 %collective-permute-start.1 = (bf16[1,3,1,176,128]{4,3,1,2,0:T(8,128)(2,1)S(1)}, bf16[1,3,1,176,128]{4,3,1,2,0:T(8,128)(2,1)S(1)}, u32[]{:S(2)}, u32[]{:S(2)}) collective-permute-start(bf16[1,3,1,176,128]{4,3,1,2,0:T(8,128)(2,1)S(1)} %fusion.83), channel_id=1, source_target_pairs={{2,0},{4,2},{6,4},{3,1},{5,3},{7,5},{10,8},{12,10},{14,12},{11,9},... | collective-permute-start | bytes 405512 | tf_op jit(solution)/shard_map/ppermute | solution.py:21
  27.8 6.0 %collective-permute-start.3 = (bf16[1,3,1,176,128]{4,3,1,2,0:T(8,128)(2,1)S(1)}, bf16[1,3,1,176,128]{4,3,1,2,0:T(8,128)(2,1)S(1)}, u32[]{:S(2)}, u32[]{:S(2)}) collective-permute-start(bf16[1,3,1,176,128]{4,3,1,2,0:T(8,128)(2,1)S(1)} %fusion.56), channel_id=1, source_target_pairs={{0,2},{2,4},{4,6},{1,3},{3,5},{5,7},{8,10},{10,12},{12,14},{9,11},... | collective-permute-start | bytes 405512 | tf_op jit(solution)/shard_map/ppermute | solution.py:19
  31.3 6.9 %collective-permute-start.4 = (bf16[1,3,1,176,128]{4,3,1,2,0:T(8,128)(2,1)S(1)}, bf16[1,3,1,176,128]{4,3,1,2,0:T(8,128)(2,1)S(1)}, u32[]{:S(2)}, u32[]{:S(2)}) collective-permute-start(bf16[1,3,1,176,128]{4,3,1,2,0:T(8,128)(2,1)S(1)} %fusion.56), channel_id=1, source_target_pairs={{2,0},{4,2},{6,4},{3,1},{5,3},{7,5},{10,8},{12,10},{14,12},{11,9},... | collective-permute-start | bytes 405512 | tf_op jit(solution)/shard_map/ppermute | solution.py:21
  39.3 6.9 %collective-permute-start.5 = (bf16[1,3,1,176,128]{4,3,1,2,0:T(8,128)(2,1)S(1)}, bf16[1,3,1,176,128]{4,3,1,2,0:T(8,128)(2,1)S(1)}, u32[]{:S(2)}, u32[]{:S(2)}) collective-permute-start(bf16[1,3,1,176,128]{4,3,1,2,0:T(8,128)(2,1)S(1)} %add_convert_fusion.5), channel_id=1, source_target_pairs={{0,8},{8,16},{16,24},{1,9},{9,17},{17,25},{2,10},{10,18},{18,26},{... | collective-permute-start | bytes 405512 | tf_op jit(solution)/shard_map/ppermute | solution.py:31
  46.3 6.0 %collective-permute-start.6 = (bf16[1,3,1,176,128]{4,3,1,2,0:T(8,128)(2,1)S(1)}, bf16[1,3,1,176,128]{4,3,1,2,0:T(8,128)(2,1)S(1)}, u32[]{:S(2)}, u32[]{:S(2)}) collective-permute-start(bf16[1,3,1,176,128]{4,3,1,2,0:T(8,128)(2,1)S(1)} %bitcast_select_fusion.16), channel_id=1, source_target_pairs={{0,2},{2,4},{4,6},{1,3},{3,5},{5,7},{8,10},{10,12},{12,14},{9,11},... | collective-permute-start | bytes 405512 | tf_op jit(solution)/shard_map/ppermute | solution.py:19
  49.8 6.9 %collective-permute-start.7 = (bf16[1,3,1,176,128]{4,3,1,2,0:T(8,128)(2,1)S(1)}, bf16[1,3,1,176,128]{4,3,1,2,0:T(8,128)(2,1)S(1)}, u32[]{:S(2)}, u32[]{:S(2)}) collective-permute-start(bf16[1,3,1,176,128]{4,3,1,2,0:T(8,128)(2,1)S(1)} %bitcast_select_fusion.16), channel_id=1, source_target_pairs={{2,0},{4,2},{6,4},{3,1},{5,3},{7,5},{10,8},{12,10},{14,12},{11,9},... | collective-permute-start | bytes 405512 | tf_op jit(solution)/shard_map/ppermute | solution.py:21
  57.8 6.9 %collective-permute-start.8 = (bf16[1,3,1,176,128]{4,3,1,2,0:T(8,128)(2,1)S(1)}, bf16[1,3,1,176,128]{4,3,1,2,0:T(8,128)(2,1)S(1)}, u32[]{:S(2)}, u32[]{:S(2)}) collective-permute-start(bf16[1,3,1,176,128]{4,3,1,2,0:T(8,128)(2,1)S(1)} %add_convert_fusion.4), channel_id=1, source_target_pairs={{0,8},{8,16},{16,24},{1,9},{9,17},{17,25},{2,10},{10,18},{18,26},{... | collective-permute-start | bytes 405512 | tf_op jit(solution)/shard_map/ppermute | solution.py:31
  64.8 6.9 %collective-permute-start.10 = (bf16[1,3,1,176,128]{4,3,1,2,0:T(8,128)(2,1)S(1)}, bf16[1,3,1,176,128]{4,3,1,2,0:T(8,128)(2,1)S(1)}, u32[]{:S(2)}, u32[]{:S(2)}) collective-permute-start(bf16[1,3,1,176,128]{4,3,1,2,0:T(8,128)(2,1)S(1)} %fusion.57), channel_id=1, source_target_pairs={{2,0},{4,2},{6,4},{3,1},{5,3},{7,5},{10,8},{12,10},{14,12},{11,9},... | collective-permute-start | bytes 405512 | tf_op jit(solution)/shard_map/ppermute | solution.py:21
  66.1 7.1 %collective-permute-start.9 = (bf16[1,3,1,176,128]{4,3,1,2,0:T(8,128)(2,1)S(1)}, bf16[1,3,1,176,128]{4,3,1,2,0:T(8,128)(2,1)S(1)}, u32[]{:S(2)}, u32[]{:S(2)}) collective-permute-start(bf16[1,3,1,176,128]{4,3,1,2,0:T(8,128)(2,1)S(1)} %fusion.57), channel_id=1, source_target_pairs={{0,2},{2,4},{4,6},{1,3},{3,5},{5,7},{8,10},{10,12},{12,14},{9,11},... | collective-permute-start | bytes 405512 | tf_op jit(solution)/shard_map/ppermute | solution.py:19
  74.4 7.7 %collective-permute-start.11 = (bf16[1,3,1,176,128]{4,3,1,2,0:T(8,128)(2,1)S(1)}, bf16[1,3,1,176,128]{4,3,1,2,0:T(8,128)(2,1)S(1)}, u32[]{:S(2)}, u32[]{:S(2)}) collective-permute-start(bf16[1,3,1,176,128]{4,3,1,2,0:T(8,128)(2,1)S(1)} %get-tuple-element.92), channel_id=1, source_target_pairs={{0,8},{8,16},{16,24},{1,9},{9,17},{17,25},{2,10},{10,18},{18,26},{... | collective-permute-start | bytes 405512 | tf_op jit(solution)/shard_map/ppermute | solution.py:31
  82.1 6.9 %collective-permute-start.12 = (bf16[1,3,1,176,128]{4,3,1,2,0:T(8,128)(2,1)S(1)}, bf16[1,3,1,176,128]{4,3,1,2,0:T(8,128)(2,1)S(1)}, u32[]{:S(2)}, u32[]{:S(2)}) collective-permute-start(bf16[1,3,1,176,128]{4,3,1,2,0:T(8,128)(2,1)S(1)} %collective-permute-done.11), channel_id=1, source_target_pairs={{0,2},{2,4},{4,6},{1,3},{3,5},{5,7},{8,10},{10,12},{12,14},{9,11},... | collective-permute-start | bytes 405512 | tf_op jit(solution)/shard_map/ppermute | solution.py:19
  86.5 6.9 %collective-permute-start.13 = (bf16[1,3,1,176,128]{4,3,1,2,0:T(8,128)(2,1)S(1)}, bf16[1,3,1,176,128]{4,3,1,2,0:T(8,128)(2,1)S(1)}, u32[]{:S(2)}, u32[]{:S(2)}) collective-permute-start(bf16[1,3,1,176,128]{4,3,1,2,0:T(8,128)(2,1)S(1)} %collective-permute-done.11), channel_id=1, source_target_pairs={{2,0},{4,2},{6,4},{3,1},{5,3},{7,5},{10,8},{12,10},{14,12},{11,9},... | collective-permute-start | bytes 405512 | tf_op jit(solution)/shard_map/ppermute | solution.py:21
  94.6 7.8 %collective-permute-start.14 = (bf16[1,3,1,176,128]{4,3,1,2,0:T(8,128)(2,1)S(1)}, bf16[1,3,1,176,128]{4,3,1,2,0:T(8,128)(2,1)S(1)}, u32[]{:S(2)}, u32[]{:S(2)}) collective-permute-start(bf16[1,3,1,176,128]{4,3,1,2,0:T(8,128)(2,1)S(1)} %get-tuple-element.90), channel_id=1, source_target_pairs={{0,8},{8,16},{16,24},{1,9},{9,17},{17,25},{2,10},{10,18},{18,26},{... | collective-permute-start | bytes 405512 | tf_op jit(solution)/shard_map/ppermute | solution.py:31
  104.3 6.9 %collective-permute-start.16 = (bf16[1,3,1,176,128]{4,3,1,2,0:T(8,128)(2,1)S(1)}, bf16[1,3,1,176,128]{4,3,1,2,0:T(8,128)(2,1)S(1)}, u32[]{:S(2)}, u32[]{:S(2)}) collective-permute-start(bf16[1,3,1,176,128]{4,3,1,2,0:T(8,128)(2,1)S(1)} %collective-permute-done.14), channel_id=1, source_target_pairs={{2,0},{4,2},{6,4},{3,1},{5,3},{7,5},{10,8},{12,10},{14,12},{11,9},... | collective-permute-start | bytes 405512 | tf_op jit(solution)/shard_map/ppermute | solution.py:21
  112.4 7.8 %collective-permute-start.17 = (bf16[1,3,1,176,128]{4,3,1,2,0:T(8,128)(2,1)S(1)}, bf16[1,3,1,176,128]{4,3,1,2,0:T(8,128)(2,1)S(1)}, u32[]{:S(2)}, u32[]{:S(2)}) collective-permute-start(bf16[1,3,1,176,128]{4,3,1,2,0:T(8,128)(2,1)S(1)} %get-tuple-element.88), channel_id=1, source_target_pairs={{0,8},{8,16},{16,24},{1,9},{9,17},{17,25},{2,10},{10,18},{18,26},{... | collective-permute-start | bytes 405512 | tf_op jit(solution)/shard_map/ppermute | solution.py:31
  122.2 6.9 %collective-permute-start.19 = (bf16[1,3,1,176,128]{4,3,1,2,0:T(8,128)(2,1)S(1)}, bf16[1,3,1,176,128]{4,3,1,2,0:T(8,128)(2,1)S(1)}, u32[]{:S(2)}, u32[]{:S(2)}) collective-permute-start(bf16[1,3,1,176,128]{4,3,1,2,0:T(8,128)(2,1)S(1)} %collective-permute-done.17), channel_id=1, source_target_pairs={{2,0},{4,2},{6,4},{3,1},{5,3},{7,5},{10,8},{12,10},{14,12},{11,9},... | collective-permute-start | bytes 405512 | tf_op jit(solution)/shard_map/ppermute | solution.py:21
  133.5 78.5 %all-to-all-start = ((s32[1,4,264,16]{2,3,0,1:T(8,128)}), s32[1,4,264,16]{2,3,0,1:T(8,128)S(1)}, u32[]{:S(2)}, u32[]{:S(2)}) async-start(s32[1,4,264,16]{2,3,0,1:T(8,128)} %copy.48), calls=%async_computation | async-start | bytes 196608 | tf_op jit(solution)/shard_map/all_to_all | solution.py:144
  212.0 32.5 %all-to-all-start.1 = ((bf16[1,4,264,16,4]{2,3,4,0,1:T(8,128)(2,1)}), bf16[1,4,264,16,4]{2,3,4,0,1:T(8,128)(2,1)S(1)}, u32[]{:S(2)}, u32[]{:S(2)}) async-start(bf16[1,4,264,16,4]{2,3,4,0,1:T(8,128)(2,1)} %copy.71), calls=%async_computation.1 | async-start | bytes 393216 | tf_op jit(solution)/shard_map/all_to_all | solution.py:143
  244.6 30.7 %all-to-all-start.2 = ((bf16[1,4,264,4,128]{4,3,2,0,1:T(4,128)(2,1)}), bf16[1,4,264,4,128]{4,3,2,0,1:T(4,128)(2,1)S(1)}, u32[]{:S(2)}, u32[]{:S(2)}) async-start(bf16[1,4,264,4,128]{4,3,2,0,1:T(4,128)(2,1)} %bitcast.70), calls=%async_computation.2 | async-start | bytes 2162688 | tf_op jit(solution)/shard_map/all_to_all | solution.py:142
  249.7 70.6 %reduce-scatter.4.cloned.1.call-start = ((), (), s32[]{:S(2)}) async-start(), calls=%async_computation.6 | async-start | bytes 737280
  288.9 6.2 %collective-permute-start.21 = (bf16[1,1,256,128]{3,2,1,0:T(8,128)(2,1)S(1)}, bf16[1,1,256,128]{3,2,1,0:T(8,128)(2,1)S(1)}, u32[]{:S(2)}, u32[]{:S(2)}) collective-permute-start(bf16[1,1,256,128]{3,2,1,0:T(8,128)(2,1)S(1)} %get-tuple-element.124), channel_id=1, source_target_pairs={{2,0},{4,2},{6,4},{3,1},{5,3},{7,5},{10,8},{12,10},{14,12},{11,9},... | collective-permute-start | bytes 196616 | tf_op jit(solution)/shard_map/ppermute | solution.py:21
  298.6 78.1 %all-reduce.16.cloned.1.call-start = ((), (), s32[]{:S(2)}) async-start(), calls=%async_computation.5 | async-start | bytes 1179648 | tf_op jit(solution)/shard_map/psum | solution.py:194
  (12 other events, 110.6 us)
Sparse Core Ops, SparseCore 0:
  131.3 46.6 all-reduce.13
  298.7 21.4 reduce-scatter.3
  323.4 53.2 all-reduce.15
where the time goes:
time: 387 us; the launch traced here: 385 us
  waiting for transfers between devices  190 us (49%)
  starting transfers between devices  77.4 us (20%)
  local copies, waits for them, and re-layouts  69.9 us (18%)
  matrix products  18.6 us (5%)
  between operations  14.9 us (4%)
  other arithmetic  14.7 us (4%)
    psum x1, waiting for transfers between devices, body(): conv_grad = lax.psum(grad_share, ('phase', 'dp'))  53 us
    psum x1, waiting for transfers between devices, from_root(): return lax.psum(block, axis)  36.8 us
    ppermute x8, waiting for transfers between devices, extended(): lax.ppermute(head, axis, [((i + 1) % count, i) for i in range(ends)])  31.1 us
    ppermute x6, starting transfers between devices, passed_along(): return lax.ppermute(block, axis, route)  27.9 us
    scatter x1, local copies, waits for them, and re-layouts, body(): send_ctx = jnp.zeros((samples_dev, tile_count * capacity, BLK, channels),...  26.7 us
    ppermute x8, starting transfers between devices, extended(): lax.ppermute(tail, axis, [(i, (i + 1) % count) for i in range(ends)])  25.9 us
    all_to_all x1, waiting for transfers between devices, body(): lax.all_to_all(send_ctx, 'tile', split_axis=1, concat_axis=1, tiled=True)  24.5 us
    unnamed x4, waiting for transfers between devices  21.6 us
  transfers between devices with their start and end apart: 28, of which 25 were waited for; matrix products, arithmetic and copies ran while one was open for 19% of the time, Pallas kernels for 0%

commit v1 on v0

--- a/solution.py
+++ b/solution.py
@@ -33,7 +33,12 @@
 
 def from_root(block, axis, source):
     block = jnp.where(lax.axis_index(axis) == source, block, jnp.zeros_like(block))
-    return lax.psum(block, axis)
+
+    def fit_modes_up(local, link_axis):
+        next_value = lax.all_gather(local, link_axis)
+        return jnp.sum(next_value, axis=0)
+
+    return fit_modes_up(block, link_axis=axis)
 
 
 def patches_from(padded, row_count, col_count):

time: 387 us -> 379 us (0.979)
  waiting for transfers between devices: 190 us -> 180 us
    psum x1 -> x0, waiting for transfers between devices: 36.8 us -> none  [from_root(): return lax.psum(block, axis)]
    all_gather x0 -> x1, waiting for transfers between devices: none -> 25.3 us  [fit_modes_up(): next_value = lax.all_gather(local, link_axis)]
    unnamed x83 -> x84, local copies, waits for them, and re-layouts: 8.65 us -> 8.68 us
  transfers between devices with their start and end apart: 28 -> 28, of which waited for: 25 -> 26; matrix products, arithmetic and copies ran while one was open for 19% -> 20% of each run, Pallas kernels for 0% -> 0%
where the time goes in v1:
time: 379 us; the launch traced here: 377 us
  waiting for transfers between devices  180 us (47%)
  starting transfers between devices  77.4 us (20%)
  local copies, waits for them, and re-layouts  69.1 us (18%)
  matrix products  18.6 us (5%)
  other arithmetic  16.7 us (4%)
  between operations  14.9 us (4%)
    psum x1, waiting for transfers between devices, body(): conv_grad = lax.psum(grad_share, ('phase', 'dp'))  53.1 us
    ppermute x8, waiting for transfers between devices, extended(): lax.ppermute(head, axis, [((i + 1) % count, i) for i in range(ends)])  30.6 us
    ppermute x6, starting transfers between devices, passed_along(): return lax.ppermute(block, axis, route)  27.9 us
    scatter x1, local copies, waits for them, and re-layouts, body(): send_ctx = jnp.zeros((samples_dev, tile_count * capacity, BLK, channels),...  26.7 us
    ppermute x8, starting transfers between devices, extended(): lax.ppermute(tail, axis, [(i, (i + 1) % count) for i in range(ends)])  25.9 us
    all_gather x1, waiting for transfers between devices, fit_modes_up(): next_value = lax.all_gather(local, link_axis)  25.3 us
    all_to_all x1, waiting for transfers between devices, body(): lax.all_to_all(send_ctx, 'tile', split_axis=1, concat_axis=1, tiled=True)  24.7 us
    unnamed x4, waiting for transfers between devices  21.4 us
  transfers between devices with their start and end apart: 28, of which 26 were waited for; matrix products, arithmetic and copies ran while one was open for 20% of the time, Pallas kernels for 0%

profile of v1, /device:TPU:0, one launch (start us, length us, event | category | flops | bytes accessed | tf_op | source)
XLA Modules:
  0.0 376.5 jit_solution(17488466689186262785)
XLA Ops:
  8.2 4.9 %collective-permute-start = (bf16[1,3,1,176,128]{4,3,1,2,0:T(8,128)(2,1)S(1)}, bf16[1,3,1,176,128]{4,3,1,2,0:T(8,128)(2,1)S(1)}, u32[]{:S(2)}, u32[]{:S(2)}) collective-permute-start(bf16[1,3,1,176,128]{4,3,1,2,0:T(8,128)(2,1)S(1)} %fusion.84), channel_id=1, source_target_pairs={{0,2},{2,4},{4,6},{1,3},{3,5},{5,7},{8,10},{10,12},{12,14},{9,11},... | collective-permute-start | bytes 405512 | tf_op jit(solution)/shard_map/ppermute | solution.py:19
  15.9 4.1 %collective-permute-done.1 = bf16[1,3,1,176,128]{4,3,1,2,0:T(8,128)(2,1)S(1)} collective-permute-done((bf16[1,3,1,176,128]{4,3,1,2,0:T(8,128)(2,1)S(1)}, bf16[1,3,1,176,128]{4,3,1,2,0:T(8,128)(2,1)S(1)}, u32[]{:S(2)}, u32[]{:S(2)}) %collective-permute-start.1) | collective-permute-done | bytes 135200 | tf_op jit(solution)/shard_map/ppermute | solution.py:21
  33.8 4.4 %collective-permute-done.4 = bf16[1,3,1,176,128]{4,3,1,2,0:T(8,128)(2,1)S(1)} collective-permute-done((bf16[1,3,1,176,128]{4,3,1,2,0:T(8,128)(2,1)S(1)}, bf16[1,3,1,176,128]{4,3,1,2,0:T(8,128)(2,1)S(1)}, u32[]{:S(2)}, u32[]{:S(2)}) %collective-permute-start.4) | collective-permute-done | bytes 135200 | tf_op jit(solution)/shard_map/ppermute | solution.py:21
  39.3 4.4 %collective-permute-start.5 = (bf16[1,3,1,176,128]{4,3,1,2,0:T(8,128)(2,1)S(1)}, bf16[1,3,1,176,128]{4,3,1,2,0:T(8,128)(2,1)S(1)}, u32[]{:S(2)}, u32[]{:S(2)}) collective-permute-start(bf16[1,3,1,176,128]{4,3,1,2,0:T(8,128)(2,1)S(1)} %add_convert_fusion.5), channel_id=1, source_target_pairs={{0,8},{8,16},{16,24},{1,9},{9,17},{17,25},{2,10},{10,18},{18,26},{... | collective-permute-start | bytes 405512 | tf_op jit(solution)/shard_map/ppermute | solution.py:31
  52.3 4.4 %collective-permute-done.7 = bf16[1,3,1,176,128]{4,3,1,2,0:T(8,128)(2,1)S(1)} collective-permute-done((bf16[1,3,1,176,128]{4,3,1,2,0:T(8,128)(2,1)S(1)}, bf16[1,3,1,176,128]{4,3,1,2,0:T(8,128)(2,1)S(1)}, u32[]{:S(2)}, u32[]{:S(2)}) %collective-permute-start.7) | collective-permute-done | bytes 135200 | tf_op jit(solution)/shard_map/ppermute | solution.py:21
  57.8 4.4 %collective-permute-start.8 = (bf16[1,3,1,176,128]{4,3,1,2,0:T(8,128)(2,1)S(1)}, bf16[1,3,1,176,128]{4,3,1,2,0:T(8,128)(2,1)S(1)}, u32[]{:S(2)}, u32[]{:S(2)}) collective-permute-start(bf16[1,3,1,176,128]{4,3,1,2,0:T(8,128)(2,1)S(1)} %add_convert_fusion.4), channel_id=1, source_target_pairs={{0,8},{8,16},{16,24},{1,9},{9,17},{17,25},{2,10},{10,18},{18,26},{... | collective-permute-start | bytes 405512 | tf_op jit(solution)/shard_map/ppermute | solution.py:31
  66.1 4.6 %collective-permute-start.9 = (bf16[1,3,1,176,128]{4,3,1,2,0:T(8,128)(2,1)S(1)}, bf16[1,3,1,176,128]{4,3,1,2,0:T(8,128)(2,1)S(1)}, u32[]{:S(2)}, u32[]{:S(2)}) collective-permute-start(bf16[1,3,1,176,128]{4,3,1,2,0:T(8,128)(2,1)S(1)} %fusion.58), channel_id=1, source_target_pairs={{0,2},{2,4},{4,6},{1,3},{3,5},{5,7},{8,10},{10,12},{12,14},{9,11},... | collective-permute-start | bytes 405512 | tf_op jit(solution)/shard_map/ppermute | solution.py:19
  74.4 5.2 %collective-permute-start.11 = (bf16[1,3,1,176,128]{4,3,1,2,0:T(8,128)(2,1)S(1)}, bf16[1,3,1,176,128]{4,3,1,2,0:T(8,128)(2,1)S(1)}, u32[]{:S(2)}, u32[]{:S(2)}) collective-permute-start(bf16[1,3,1,176,128]{4,3,1,2,0:T(8,128)(2,1)S(1)} %get-tuple-element.92), channel_id=1, source_target_pairs={{0,8},{8,16},{16,24},{1,9},{9,17},{17,25},{2,10},{10,18},{18,26},{... | collective-permute-start | bytes 405512 | tf_op jit(solution)/shard_map/ppermute | solution.py:31
  82.1 4.4 %collective-permute-start.12 = (bf16[1,3,1,176,128]{4,3,1,2,0:T(8,128)(2,1)S(1)}, bf16[1,3,1,176,128]{4,3,1,2,0:T(8,128)(2,1)S(1)}, u32[]{:S(2)}, u32[]{:S(2)}) collective-permute-start(bf16[1,3,1,176,128]{4,3,1,2,0:T(8,128)(2,1)S(1)} %collective-permute-done.11), channel_id=1, source_target_pairs={{0,2},{2,4},{4,6},{1,3},{3,5},{5,7},{8,10},{10,12},{12,14},{9,11},... | collective-permute-start | bytes 405512 | tf_op jit(solution)/shard_map/ppermute | solution.py:19
  89.0 4.4 %collective-permute-done.13 = bf16[1,3,1,176,128]{4,3,1,2,0:T(8,128)(2,1)S(1)} collective-permute-done((bf16[1,3,1,176,128]{4,3,1,2,0:T(8,128)(2,1)S(1)}, bf16[1,3,1,176,128]{4,3,1,2,0:T(8,128)(2,1)S(1)}, u32[]{:S(2)}, u32[]{:S(2)}) %collective-permute-start.13) | collective-permute-done | bytes 135200 | tf_op jit(solution)/shard_map/ppermute | solution.py:21
  94.6 5.3 %collective-permute-start.14 = (bf16[1,3,1,176,128]{4,3,1,2,0:T(8,128)(2,1)S(1)}, bf16[1,3,1,176,128]{4,3,1,2,0:T(8,128)(2,1)S(1)}, u32[]{:S(2)}, u32[]{:S(2)}) collective-permute-start(bf16[1,3,1,176,128]{4,3,1,2,0:T(8,128)(2,1)S(1)} %get-tuple-element.90), channel_id=1, source_target_pairs={{0,8},{8,16},{16,24},{1,9},{9,17},{17,25},{2,10},{10,18},{18,26},{... | collective-permute-start | bytes 405512 | tf_op jit(solution)/shard_map/ppermute | solution.py:31
  106.8 4.4 %collective-permute-done.16 = bf16[1,3,1,176,128]{4,3,1,2,0:T(8,128)(2,1)S(1)} collective-permute-done((bf16[1,3,1,176,128]{4,3,1,2,0:T(8,128)(2,1)S(1)}, bf16[1,3,1,176,128]{4,3,1,2,0:T(8,128)(2,1)S(1)}, u32[]{:S(2)}, u32[]{:S(2)}) %collective-permute-start.16) | collective-permute-done | bytes 135200 | tf_op jit(solution)/shard_map/ppermute | solution.py:21
  112.4 5.3 %collective-permute-start.17 = (bf16[1,3,1,176,128]{4,3,1,2,0:T(8,128)(2,1)S(1)}, bf16[1,3,1,176,128]{4,3,1,2,0:T(8,128)(2,1)S(1)}, u32[]{:S(2)}, u32[]{:S(2)}) collective-permute-start(bf16[1,3,1,176,128]{4,3,1,2,0:T(8,128)(2,1)S(1)} %get-tuple-element.88), channel_id=1, source_target_pairs={{0,8},{8,16},{16,24},{1,9},{9,17},{17,25},{2,10},{10,18},{18,26},{... | collective-permute-start | bytes 405512 | tf_op jit(solution)/shard_map/ppermute | solution.py:31
  142.8 25.3 %all-gather.3.cloned.1.call-done = bf16[16,1,3,1,176,128]{5,4,3,2,1,0:T(8,128)(2,1)} async-done(((bf16[4,1,3,1,176,128]{5,4,3,2,1,0:T(8,128)(2,1)}), bf16[16,1,3,1,176,128]{5,4,3,2,1,0:T(8,128)(2,1)}) %all-gather.3.cloned.1.call-update) | async-done | bytes 2162704 | tf_op jit(solution)/shard_map/all_gather | solution.py:38
  171.4 7.7 %fusion.26 = (bf16[132,2,4]{2,1,0:T(2,128)(2,1)S(1)}, bf16[132,2,4]{2,1,0:T(2,128)(2,1)S(1)}, bf16[132,2,4]{2,1,0:T(2,128)(2,1)S(1)}, bf16[132,2,4]{2,1,0:T(2,12...) fusion(pred[1,132,2,4,59]{4,3,2,1,0:T(4,128)(4,1)S(1)} %eq.411,, ...), kind=kLoop, calls=%fused_computation.54 | loop fusion | flops 1976832 | bytes 1279872 | tf_op jit(solution)/shard_map/reduce_sum | solution.py:108
  193.4 8.6 %scatter_fusion = bf16[1056,16,4]{1,2,0:T(4,128)(2,1)S(1)} fusion(bf16[1056,16,4]{1,2,0:T(4,128)(2,1)S(1)} %broadcast.618, s32[264]{0:T(512)S(1)} %fusion.63, bf16[264,16,4]{1,2,0:T(4,128)(2,1)S(1)} %copy.72), kind=kCustom, calls=%fused_computation.1 | custom fusion | bytes 102432 | tf_op jit(solution)/shard_map/scatter | solution.py:136
  203.3 4.6 %all-to-all-start.1 = ((bf16[1,4,264,16,4]{2,3,4,0,1:T(8,128)(2,1)}), bf16[1,4,264,16,4]{2,3,4,0,1:T(8,128)(2,1)S(1)}, u32[]{:S(2)}, u32[]{:S(2)}) async-start(bf16[1,4,264,16,4]{2,3,4,0,1:T(8,128)(2,1)} %copy.73), calls=%async_computation.1 | async-start | bytes 393216 | tf_op jit(solution)/shard_map/all_to_all | solution.py:148
  209.1 26.7 %scatter_fusion.1 = bf16[1056,4,128]{2,1,0:T(4,128)(2,1)} fusion(bf16[1056,4,128]{2,1,0:T(4,128)(2,1)} %broadcast.620, s32[264]{0:T(512)S(1)} %fusion.63, bf16[264,4,128]{2,1,0:T(4,128)(2,1)S(1)} %bitcast.280), kind=kCustom, calls=%fused_computation.2 | custom fusion | bytes 812064 | tf_op jit(solution)/shard_map/scatter | solution.py:131
  235.8 5.1 %all-to-all-start.2 = ((bf16[1,4,264,4,128]{4,3,2,0,1:T(4,128)(2,1)}), bf16[1,4,264,4,128]{4,3,2,0,1:T(4,128)(2,1)S(1)}, u32[]{:S(2)}, u32[]{:S(2)}) async-start(bf16[1,4,264,4,128]{4,3,2,0,1:T(4,128)(2,1)} %bitcast.73), calls=%async_computation.2 | async-start | bytes 2162688 | tf_op jit(solution)/shard_map/all_to_all | solution.py:147
  242.0 24.7 %all-to-all-done.2 = bf16[1,4,264,4,128]{4,3,2,0,1:T(4,128)(2,1)S(1)} async-done(((bf16[1,4,264,4,128]{4,3,2,0,1:T(4,128)(2,1)}), bf16[1,4,264,4,128]{4,3,2,0,1:T(4,128)(2,1)S(1)}, u32[]{:S(2)}, u32[]{:S(2)}) %all-to-all-start.2) | async-done | bytes 1081376 | tf_op jit(solution)/shard_map/all_to_all | solution.py:147
  268.5 10.5 %fusion.4 = bf16[1024,128]{1,0:T(8,128)(2,1)S(1)} fusion(bf16[16896,128]{1,0:T(8,128)(2,1)S(1)} %bitcast.252, s32[16896]{0:T(1024)S(1)} %eq.358), kind=kOutput, calls=%fused_computation.15 | convolution fusion | flops 4446617600 | bytes 4655104 | tf_op jit(solution)/shard_map/while/body/eval_jaxpr/sxr,src->sxc/dot_general | solution.py:166
  282.2 4.3 %collective-permute-done.21 = bf16[1,1,256,128]{3,2,1,0:T(8,128)(2,1)S(1)} collective-permute-done((bf16[1,1,256,128]{3,2,1,0:T(8,128)(2,1)S(1)}, bf16[1,1,256,128]{3,2,1,0:T(8,128)(2,1)S(1)}, u32[]{:S(2)}, u32[]{:S(2)}) %collective-permute-start.21) | collective-permute-done | bytes 65568 | tf_op jit(solution)/shard_map/ppermute | solution.py:21
  290.1 21.3 %reduce-scatter.4.cloned.1.call-done = f32[32,1152]{1,0:T(8,128)} async-done(((f32[128,1152]{1,0:T(8,128)}), f32[32,1152]{1,0:T(8,128)}) %reduce-scatter.4.cloned.1.call-update) | async-done | bytes 147472
  314.9 53.1 %all-reduce.13.cloned.1.call-done = f32[32,1152]{0,1:T(8,128)} async-done(((f32[32,1152]{0,1:T(8,128)}), f32[32,1152]{0,1:T(8,128)}) %all-reduce.13.cloned.1.call-update) | async-done | bytes 147472 | tf_op jit(solution)/shard_map/psum | solution.py:199
  (234 shorter events, 109.7 us)
Async XLA Ops:
  7.2 161.0 %all-gather.3.cloned.1.call-start = ((), (), s32[]{:S(2)}) async-start(), calls=%async_computation.5 | async-start | bytes 2703360 | tf_op jit(solution)/shard_map/all_gather | solution.py:38
  8.2 7.8 %collective-permute-start = (bf16[1,3,1,176,128]{4,3,1,2,0:T(8,128)(2,1)S(1)}, bf16[1,3,1,176,128]{4,3,1,2,0:T(8,128)(2,1)S(1)}, u32[]{:S(2)}, u32[]{:S(2)}) collective-permute-start(bf16[1,3,1,176,128]{4,3,1,2,0:T(8,128)(2,1)S(1)} %fusion.84), channel_id=1, source_target_pairs={{0,2},{2,4},{4,6},{1,3},{3,5},{5,7},{8,10},{10,12},{12,14},{9,11},... | collective-permute-start | bytes 405512 | tf_op jit(solution)/shard_map/ppermute | solution.py:19
  13.1 6.9 %collective-permute-start.1 = (bf16[1,3,1,176,128]{4,3,1,2,0:T(8,128)(2,1)S(1)}, bf16[1,3,1,176,128]{4,3,1,2,0:T(8,128)(2,1)S(1)}, u32[]{:S(2)}, u32[]{:S(2)}) collective-permute-start(bf16[1,3,1,176,128]{4,3,1,2,0:T(8,128)(2,1)S(1)} %fusion.84), channel_id=1, source_target_pairs={{2,0},{4,2},{6,4},{3,1},{5,3},{7,5},{10,8},{12,10},{14,12},{11,9},... | collective-permute-start | bytes 405512 | tf_op jit(solution)/shard_map/ppermute | solution.py:21
  27.8 6.0 %collective-permute-start.3 = (bf16[1,3,1,176,128]{4,3,1,2,0:T(8,128)(2,1)S(1)}, bf16[1,3,1,176,128]{4,3,1,2,0:T(8,128)(2,1)S(1)}, u32[]{:S(2)}, u32[]{:S(2)}) collective-permute-start(bf16[1,3,1,176,128]{4,3,1,2,0:T(8,128)(2,1)S(1)} %fusion.56), channel_id=1, source_target_pairs={{0,2},{2,4},{4,6},{1,3},{3,5},{5,7},{8,10},{10,12},{12,14},{9,11},... | collective-permute-start | bytes 405512 | tf_op jit(solution)/shard_map/ppermute | solution.py:19
  31.3 6.9 %collective-permute-start.4 = (bf16[1,3,1,176,128]{4,3,1,2,0:T(8,128)(2,1)S(1)}, bf16[1,3,1,176,128]{4,3,1,2,0:T(8,128)(2,1)S(1)}, u32[]{:S(2)}, u32[]{:S(2)}) collective-permute-start(bf16[1,3,1,176,128]{4,3,1,2,0:T(8,128)(2,1)S(1)} %fusion.56), channel_id=1, source_target_pairs={{2,0},{4,2},{6,4},{3,1},{5,3},{7,5},{10,8},{12,10},{14,12},{11,9},... | collective-permute-start | bytes 405512 | tf_op jit(solution)/shard_map/ppermute | solution.py:21
  39.3 6.9 %collective-permute-start.5 = (bf16[1,3,1,176,128]{4,3,1,2,0:T(8,128)(2,1)S(1)}, bf16[1,3,1,176,128]{4,3,1,2,0:T(8,128)(2,1)S(1)}, u32[]{:S(2)}, u32[]{:S(2)}) collective-permute-start(bf16[1,3,1,176,128]{4,3,1,2,0:T(8,128)(2,1)S(1)} %add_convert_fusion.5), channel_id=1, source_target_pairs={{0,8},{8,16},{16,24},{1,9},{9,17},{17,25},{2,10},{10,18},{18,26},{... | collective-permute-start | bytes 405512 | tf_op jit(solution)/shard_map/ppermute | solution.py:31
  46.3 6.0 %collective-permute-start.6 = (bf16[1,3,1,176,128]{4,3,1,2,0:T(8,128)(2,1)S(1)}, bf16[1,3,1,176,128]{4,3,1,2,0:T(8,128)(2,1)S(1)}, u32[]{:S(2)}, u32[]{:S(2)}) collective-permute-start(bf16[1,3,1,176,128]{4,3,1,2,0:T(8,128)(2,1)S(1)} %fusion.57), channel_id=1, source_target_pairs={{0,2},{2,4},{4,6},{1,3},{3,5},{5,7},{8,10},{10,12},{12,14},{9,11},... | collective-permute-start | bytes 405512 | tf_op jit(solution)/shard_map/ppermute | solution.py:19
  49.8 6.9 %collective-permute-start.7 = (bf16[1,3,1,176,128]{4,3,1,2,0:T(8,128)(2,1)S(1)}, bf16[1,3,1,176,128]{4,3,1,2,0:T(8,128)(2,1)S(1)}, u32[]{:S(2)}, u32[]{:S(2)}) collective-permute-start(bf16[1,3,1,176,128]{4,3,1,2,0:T(8,128)(2,1)S(1)} %fusion.57), channel_id=1, source_target_pairs={{2,0},{4,2},{6,4},{3,1},{5,3},{7,5},{10,8},{12,10},{14,12},{11,9},... | collective-permute-start | bytes 405512 | tf_op jit(solution)/shard_map/ppermute | solution.py:21
  57.8 6.9 %collective-permute-start.8 = (bf16[1,3,1,176,128]{4,3,1,2,0:T(8,128)(2,1)S(1)}, bf16[1,3,1,176,128]{4,3,1,2,0:T(8,128)(2,1)S(1)}, u32[]{:S(2)}, u32[]{:S(2)}) collective-permute-start(bf16[1,3,1,176,128]{4,3,1,2,0:T(8,128)(2,1)S(1)} %add_convert_fusion.4), channel_id=1, source_target_pairs={{0,8},{8,16},{16,24},{1,9},{9,17},{17,25},{2,10},{10,18},{18,26},{... | collective-permute-start | bytes 405512 | tf_op jit(solution)/shard_map/ppermute | solution.py:31
  64.8 6.9 %collective-permute-start.10 = (bf16[1,3,1,176,128]{4,3,1,2,0:T(8,128)(2,1)S(1)}, bf16[1,3,1,176,128]{4,3,1,2,0:T(8,128)(2,1)S(1)}, u32[]{:S(2)}, u32[]{:S(2)}) collective-permute-start(bf16[1,3,1,176,128]{4,3,1,2,0:T(8,128)(2,1)S(1)} %fusion.58), channel_id=1, source_target_pairs={{2,0},{4,2},{6,4},{3,1},{5,3},{7,5},{10,8},{12,10},{14,12},{11,9},... | collective-permute-start | bytes 405512 | tf_op jit(solution)/shard_map/ppermute | solution.py:21
  66.1 7.1 %collective-permute-start.9 = (bf16[1,3,1,176,128]{4,3,1,2,0:T(8,128)(2,1)S(1)}, bf16[1,3,1,176,128]{4,3,1,2,0:T(8,128)(2,1)S(1)}, u32[]{:S(2)}, u32[]{:S(2)}) collective-permute-start(bf16[1,3,1,176,128]{4,3,1,2,0:T(8,128)(2,1)S(1)} %fusion.58), channel_id=1, source_target_pairs={{0,2},{2,4},{4,6},{1,3},{3,5},{5,7},{8,10},{10,12},{12,14},{9,11},... | collective-permute-start | bytes 405512 | tf_op jit(solution)/shard_map/ppermute | solution.py:19
  74.4 7.7 %collective-permute-start.11 = (bf16[1,3,1,176,128]{4,3,1,2,0:T(8,128)(2,1)S(1)}, bf16[1,3,1,176,128]{4,3,1,2,0:T(8,128)(2,1)S(1)}, u32[]{:S(2)}, u32[]{:S(2)}) collective-permute-start(bf16[1,3,1,176,128]{4,3,1,2,0:T(8,128)(2,1)S(1)} %get-tuple-element.92), channel_id=1, source_target_pairs={{0,8},{8,16},{16,24},{1,9},{9,17},{17,25},{2,10},{10,18},{18,26},{... | collective-permute-start | bytes 405512 | tf_op jit(solution)/shard_map/ppermute | solution.py:31
  82.1 6.9 %collective-permute-start.12 = (bf16[1,3,1,176,128]{4,3,1,2,0:T(8,128)(2,1)S(1)}, bf16[1,3,1,176,128]{4,3,1,2,0:T(8,128)(2,1)S(1)}, u32[]{:S(2)}, u32[]{:S(2)}) collective-permute-start(bf16[1,3,1,176,128]{4,3,1,2,0:T(8,128)(2,1)S(1)} %collective-permute-done.11), channel_id=1, source_target_pairs={{0,2},{2,4},{4,6},{1,3},{3,5},{5,7},{8,10},{10,12},{12,14},{9,11},... | collective-permute-start | bytes 405512 | tf_op jit(solution)/shard_map/ppermute | solution.py:19
  86.5 6.9 %collective-permute-start.13 = (bf16[1,3,1,176,128]{4,3,1,2,0:T(8,128)(2,1)S(1)}, bf16[1,3,1,176,128]{4,3,1,2,0:T(8,128)(2,1)S(1)}, u32[]{:S(2)}, u32[]{:S(2)}) collective-permute-start(bf16[1,3,1,176,128]{4,3,1,2,0:T(8,128)(2,1)S(1)} %collective-permute-done.11), channel_id=1, source_target_pairs={{2,0},{4,2},{6,4},{3,1},{5,3},{7,5},{10,8},{12,10},{14,12},{11,9},... | collective-permute-start | bytes 405512 | tf_op jit(solution)/shard_map/ppermute | solution.py:21
  94.6 7.8 %collective-permute-start.14 = (bf16[1,3,1,176,128]{4,3,1,2,0:T(8,128)(2,1)S(1)}, bf16[1,3,1,176,128]{4,3,1,2,0:T(8,128)(2,1)S(1)}, u32[]{:S(2)}, u32[]{:S(2)}) collective-permute-start(bf16[1,3,1,176,128]{4,3,1,2,0:T(8,128)(2,1)S(1)} %get-tuple-element.90), channel_id=1, source_target_pairs={{0,8},{8,16},{16,24},{1,9},{9,17},{17,25},{2,10},{10,18},{18,26},{... | collective-permute-start | bytes 405512 | tf_op jit(solution)/shard_map/ppermute | solution.py:31
  104.3 6.9 %collective-permute-start.16 = (bf16[1,3,1,176,128]{4,3,1,2,0:T(8,128)(2,1)S(1)}, bf16[1,3,1,176,128]{4,3,1,2,0:T(8,128)(2,1)S(1)}, u32[]{:S(2)}, u32[]{:S(2)}) collective-permute-start(bf16[1,3,1,176,128]{4,3,1,2,0:T(8,128)(2,1)S(1)} %collective-permute-done.14), channel_id=1, source_target_pairs={{2,0},{4,2},{6,4},{3,1},{5,3},{7,5},{10,8},{12,10},{14,12},{11,9},... | collective-permute-start | bytes 405512 | tf_op jit(solution)/shard_map/ppermute | solution.py:21
  112.4 7.8 %collective-permute-start.17 = (bf16[1,3,1,176,128]{4,3,1,2,0:T(8,128)(2,1)S(1)}, bf16[1,3,1,176,128]{4,3,1,2,0:T(8,128)(2,1)S(1)}, u32[]{:S(2)}, u32[]{:S(2)}) collective-permute-start(bf16[1,3,1,176,128]{4,3,1,2,0:T(8,128)(2,1)S(1)} %get-tuple-element.88), channel_id=1, source_target_pairs={{0,8},{8,16},{16,24},{1,9},{9,17},{17,25},{2,10},{10,18},{18,26},{... | collective-permute-start | bytes 405512 | tf_op jit(solution)/shard_map/ppermute | solution.py:31
  122.1 7.0 %collective-permute-start.19 = (bf16[1,3,1,176,128]{4,3,1,2,0:T(8,128)(2,1)S(1)}, bf16[1,3,1,176,128]{4,3,1,2,0:T(8,128)(2,1)S(1)}, u32[]{:S(2)}, u32[]{:S(2)}) collective-permute-start(bf16[1,3,1,176,128]{4,3,1,2,0:T(8,128)(2,1)S(1)} %collective-permute-done.17), channel_id=1, source_target_pairs={{2,0},{4,2},{6,4},{3,1},{5,3},{7,5},{10,8},{12,10},{14,12},{11,9},... | collective-permute-start | bytes 405512 | tf_op jit(solution)/shard_map/ppermute | solution.py:21
  135.2 68.1 %all-to-all-start = ((s32[1,4,264,16]{2,3,0,1:T(8,128)}), s32[1,4,264,16]{2,3,0,1:T(8,128)S(1)}, u32[]{:S(2)}, u32[]{:S(2)}) async-start(s32[1,4,264,16]{2,3,0,1:T(8,128)} %copy.48), calls=%async_computation | async-start | bytes 196608 | tf_op jit(solution)/shard_map/all_to_all | solution.py:149
  203.3 32.5 %all-to-all-start.1 = ((bf16[1,4,264,16,4]{2,3,4,0,1:T(8,128)(2,1)}), bf16[1,4,264,16,4]{2,3,4,0,1:T(8,128)(2,1)S(1)}, u32[]{:S(2)}, u32[]{:S(2)}) async-start(bf16[1,4,264,16,4]{2,3,4,0,1:T(8,128)(2,1)} %copy.73), calls=%async_computation.1 | async-start | bytes 393216 | tf_op jit(solution)/shard_map/all_to_all | solution.py:148
  235.8 30.9 %all-to-all-start.2 = ((bf16[1,4,264,4,128]{4,3,2,0,1:T(4,128)(2,1)}), bf16[1,4,264,4,128]{4,3,2,0,1:T(4,128)(2,1)S(1)}, u32[]{:S(2)}, u32[]{:S(2)}) async-start(bf16[1,4,264,4,128]{4,3,2,0,1:T(4,128)(2,1)} %bitcast.73), calls=%async_computation.2 | async-start | bytes 2162688 | tf_op jit(solution)/shard_map/all_to_all | solution.py:147
  240.9 70.5 %reduce-scatter.4.cloned.1.call-start = ((), (), s32[]{:S(2)}) async-start(), calls=%async_computation.6 | async-start | bytes 737280
  280.3 6.2 %collective-permute-start.21 = (bf16[1,1,256,128]{3,2,1,0:T(8,128)(2,1)S(1)}, bf16[1,1,256,128]{3,2,1,0:T(8,128)(2,1)S(1)}, u32[]{:S(2)}, u32[]{:S(2)}) collective-permute-start(bf16[1,1,256,128]{3,2,1,0:T(8,128)(2,1)S(1)} %get-tuple-element.124), channel_id=1, source_target_pairs={{2,0},{4,2},{6,4},{3,1},{5,3},{7,5},{10,8},{12,10},{14,12},{11,9},... | collective-permute-start | bytes 196616 | tf_op jit(solution)/shard_map/ppermute | solution.py:21
  290.1 78.0 %all-reduce.13.cloned.1.call-start = ((), (), s32[]{:S(2)}) async-start(), calls=%async_computation.4 | async-start | bytes 1179648 | tf_op jit(solution)/shard_map/psum | solution.py:199
  (12 other events, 70.8 us)
Sparse Core Ops, SparseCore 0:
  131.4 36.7 all-gather.2
  290.2 21.2 reduce-scatter.3
  314.6 53.3 all-reduce.12
